TPU v7x, 512 devices: a whole 4x4x16 slice. The times are simulated.
512 devices in a mesh: cd: 32 (over z_hi, y, x), ab: 16 (over z_lo, core).
Axes of the slice: x: 4, y: 4, z: 16 (z_hi: 2, z_lo: 8; z = z_hi * 8 + z_lo), core: 2. Of those that a mesh axis runs over, the one named last changes fastest.
Arguments:
- amplitudes: float32 [384, 65536], P('ab', 'cd'), may hold values from -6 to 6
- integrals: float32 [65536, 8192], P('cd', 'ab'), may hold values from -0.046875 to 0.046875
- residual_in: float32 [384, 8192], P('cd', 'ab'), may hold values from -6 to 6
- pair_irrep_ij: int32 [384], P('ab'), may hold values from 0 to 3
- pair_irrep_cd: int32 [65536], P('cd'), may hold values from 0 to 3
- pair_irrep_ab: int32 [8192], P('ab'), may hold values from 0 to 3
Outputs:
- residual_out: float32 [384, 8192], P('cd', 'ab')
All inputs are finite; a program needn't handle non-finite values.
Results may differ from a plain program's by a relative error of at most 0.0003.
Values sent between devices are 32-bit elements; how exact they have to be, the bound alone decides.
A program may use at most 64 MiB of HBM per device.

v0:
```python
import jax
import jax.numpy as jnp
from jax import lax
from jax.sharding import PartitionSpec as P


def body(amplitudes, integrals, residual_in, pair_irrep_ij, pair_irrep_cd, pair_irrep_ab):
    masked_t2 = jnp.where(
        pair_irrep_ij[:, None] == pair_irrep_cd[None, :], amplitudes, jnp.zeros_like(amplitudes)
    )
    masked_v = jnp.where(
        pair_irrep_cd[:, None] == pair_irrep_ab[None, :], integrals, jnp.zeros_like(integrals)
    )
    partial_sum = jnp.dot(
        lax.all_gather(masked_t2, "ab", axis=0, tiled=True),
        masked_v,
        precision=lax.Precision.HIGHEST,
        preferred_element_type=jnp.float32,
    )
    share = lax.psum_scatter(partial_sum, "cd", scatter_dimension=0, tiled=True)
    return residual_in + share


def solution(mesh):
    placed = (P("ab", "cd"), P("cd", "ab"), P("cd", "ab"), P("ab"), P("cd"), P("ab"))
    return jax.shard_map(body, mesh=mesh, in_specs=placed, out_specs=P("cd", "ab"), check_vma=False)
```

profile of v0, /device:TPU:20, one launch (start us, length us, event | category | flops | bytes accessed | tf_op | source)
XLA Modules:
  0.0 340.5 jit_solution(17492330742637534261)
XLA Ops:
  6.5 0.0 all-gather.2.cloned.1.call-start
  6.5 1.7 compare_select_fusion
  8.2 0.0 all-gather.2.cloned.1.call-update
  8.3 0.0 copy-start
  8.3 109.3 %all-gather.2.cloned.1.call-done = f32[384,2048]{1,0:T(8,128)} async-done(((f32[24,2048]{1,0:T(8,128)}), f32[384,2048]{1,0:T(8,128)}) %all-gather.2.cloned.1.call-update) | async-done | bytes 3145744 | tf_op jit(solution)/shard_map/all_gather | solution.py:15
  117.6 8.5 %fusion.1 = f32[384,512]{1,0:T(8,128)S(1)} fusion(f32[384,2048]{1,0:T(8,128)} %all-gather.2.cloned.1.call-done, f32[2048,512]{1,0:T(8,128)} %param.7, s32[512]{0:T(512)} %param.11, s32[2048]{0:T(1024)} %param.10), kind=kOutput, calls=%fused_computation | convolution fusion | flops 4833935360 | bytes 8136704 | tf_op jit(solution)/shard_map/dot_general | solution.py:14
  126.1 127.7 %fusion = f32[16,512]{1,0:T(8,128)S(1)} fusion(f32[384,512]{1,0:T(8,128)S(1)} %fusion.1), kind=kCustom, calls=%all-reduce-scatter | all-reduce-scatter fusion | flops 262145 | bytes 821248
  253.9 4.8 %collective-permute-start = (f32[16,512]{1,0:T(8,128)S(1)}, f32[16,512]{1,0:T(8,128)S(1)}, u32[]{:S(2)}, u32[]{:S(2)}) collective-permute-start(f32[16,512]{1,0:T(8,128)S(1)} %fusion), channel_id=1, source_target_pairs={{0,16},{16,32},{32,48},{48,64},{64,80},{80,96},{96,112},{112,128},... | collective-permute-start | bytes 98312
  258.6 15.7 %collective-permute-start.1 = (f32[16,512]{1,0:T(8,128)S(1)}, f32[16,512]{1,0:T(8,128)S(1)}, u32[]{:S(2)}, u32[]{:S(2)}) collective-permute-start(f32[16,512]{1,0:T(8,128)S(1)} %fusion), channel_id=1, source_target_pairs={{0,32},{16,48},{32,64},{48,80},{64,96},{80,112},{96,128},{112,144}... | collective-permute-start | bytes 98312
  274.4 13.0 %collective-permute-start.7 = (f32[12,512]{1,0:T(8,128)S(1)}, f32[12,512]{1,0:T(8,128)S(1)}, u32[]{:S(2)}, u32[]{:S(2)}) collective-permute-start(f32[12,512]{1,0:T(8,128)S(1)} %slice), channel_id=1, source_target_pairs={{0,128},{16,144},{32,160},{48,176},{64,192},{80,208},{96,224},{112... | collective-permute-start | bytes 73736
  287.4 19.2 %collective-permute-start.2 = (f32[16,512]{1,0:T(8,128)S(1)}, f32[16,512]{1,0:T(8,128)S(1)}, u32[]{:S(2)}, u32[]{:S(2)}) collective-permute-start(f32[16,512]{1,0:T(8,128)S(1)} %fusion), channel_id=1, source_target_pairs={{0,48},{16,64},{32,80},{48,96},{64,112},{80,128},{96,144},{112,160... | collective-permute-start | bytes 98312
  306.6 1.9 collective-permute-start.3
  308.5 0.0 collective-permute-done.7
  308.5 2.0 collective-permute-start.4
  310.5 0.0 collective-permute-done
  310.5 13.3 %collective-permute-start.5 = (f32[16,512]{1,0:T(8,128)S(1)}, f32[16,512]{1,0:T(8,128)S(1)}, u32[]{:S(2)}, u32[]{:S(2)}) collective-permute-start(f32[16,512]{1,0:T(8,128)S(1)} %fusion), channel_id=1, source_target_pairs={{0,96},{16,112},{32,128},{48,144},{64,160},{80,176},{96,192},{112,... | collective-permute-start | bytes 98312
  323.8 0.0 collective-permute-done.1
  323.8 1.9 collective-permute-start.6
  325.7 1.3 dynamic-slice.4
  327.6 0.0 collective-permute-done.2
  327.6 0.0 collective-permute-done.3
  327.7 0.0 collective-permute-done.4
  327.7 0.0 collective-permute-done.5
  327.7 4.3 %collective-permute-done.6 = f32[16,512]{1,0:T(8,128)S(1)} collective-permute-done((f32[16,512]{1,0:T(8,128)S(1)}, f32[16,512]{1,0:T(8,128)S(1)}, u32[]{:S(2)}, u32[]{:S(2)}) %collective-permute-start.6) | collective-permute-done | bytes 32800
  332.0 1.0 concatenate
  333.0 0.0 copy-done
  333.0 0.6 dynamic-slice_add_fusion
  (1 shorter events, 0.0 us)
Async XLA Ops:
  6.5 111.0 %all-gather.2.cloned.1.call-start = ((), (), s32[]{:S(2)}) async-start(), calls=%async_computation | async-start | bytes 3342336 | tf_op jit(solution)/shard_map/all_gather | solution.py:15
  8.3 324.7 %copy-start = (f32[12,512]{1,0:T(8,128)S(1)}, f32[12,512]{1,0:T(8,128)}, u32[]{:S(2)}) copy-start(f32[12,512]{1,0:T(8,128)} %param.8) | copy-start | bytes 73732
  253.9 56.6 %collective-permute-start = (f32[16,512]{1,0:T(8,128)S(1)}, f32[16,512]{1,0:T(8,128)S(1)}, u32[]{:S(2)}, u32[]{:S(2)}) collective-permute-start(f32[16,512]{1,0:T(8,128)S(1)} %fusion), channel_id=1, source_target_pairs={{0,16},{16,32},{32,48},{48,64},{64,80},{80,96},{96,112},{112,128},... | collective-permute-start | bytes 98312
  258.6 65.1 %collective-permute-start.1 = (f32[16,512]{1,0:T(8,128)S(1)}, f32[16,512]{1,0:T(8,128)S(1)}, u32[]{:S(2)}, u32[]{:S(2)}) collective-permute-start(f32[16,512]{1,0:T(8,128)S(1)} %fusion), channel_id=1, source_target_pairs={{0,32},{16,48},{32,64},{48,80},{64,96},{80,112},{96,128},{112,144}... | collective-permute-start | bytes 98312
  274.4 34.1 %collective-permute-start.7 = (f32[12,512]{1,0:T(8,128)S(1)}, f32[12,512]{1,0:T(8,128)S(1)}, u32[]{:S(2)}, u32[]{:S(2)}) collective-permute-start(f32[12,512]{1,0:T(8,128)S(1)} %slice), channel_id=1, source_target_pairs={{0,128},{16,144},{32,160},{48,176},{64,192},{80,208},{96,224},{112... | collective-permute-start | bytes 73736
  287.4 40.2 %collective-permute-start.2 = (f32[16,512]{1,0:T(8,128)S(1)}, f32[16,512]{1,0:T(8,128)S(1)}, u32[]{:S(2)}, u32[]{:S(2)}) collective-permute-start(f32[16,512]{1,0:T(8,128)S(1)} %fusion), channel_id=1, source_target_pairs={{0,48},{16,64},{32,80},{48,96},{64,112},{80,128},{96,144},{112,160... | collective-permute-start | bytes 98312
  306.6 21.1 %collective-permute-start.3 = (f32[16,512]{1,0:T(8,128)S(1)}, f32[16,512]{1,0:T(8,128)S(1)}, u32[]{:S(2)}, u32[]{:S(2)}) collective-permute-start(f32[16,512]{1,0:T(8,128)S(1)} %fusion), channel_id=1, source_target_pairs={{0,64},{16,80},{32,96},{48,112},{64,128},{80,144},{96,160},{112,17... | collective-permute-start | bytes 98312
  308.5 19.2 %collective-permute-start.4 = (f32[16,512]{1,0:T(8,128)S(1)}, f32[16,512]{1,0:T(8,128)S(1)}, u32[]{:S(2)}, u32[]{:S(2)}) collective-permute-start(f32[16,512]{1,0:T(8,128)S(1)} %fusion), channel_id=1, source_target_pairs={{0,80},{16,96},{32,112},{48,128},{64,144},{80,160},{96,176},{112,1... | collective-permute-start | bytes 98312
  310.5 17.2 %collective-permute-start.5 = (f32[16,512]{1,0:T(8,128)S(1)}, f32[16,512]{1,0:T(8,128)S(1)}, u32[]{:S(2)}, u32[]{:S(2)}) collective-permute-start(f32[16,512]{1,0:T(8,128)S(1)} %fusion), channel_id=1, source_target_pairs={{0,96},{16,112},{32,128},{48,144},{64,160},{80,176},{96,192},{112,... | collective-permute-start | bytes 98312
  323.8 8.2 %collective-permute-start.6 = (f32[16,512]{1,0:T(8,128)S(1)}, f32[16,512]{1,0:T(8,128)S(1)}, u32[]{:S(2)}, u32[]{:S(2)}) collective-permute-start(f32[16,512]{1,0:T(8,128)S(1)} %fusion), channel_id=1, source_target_pairs={{0,112},{16,128},{32,144},{48,160},{64,176},{80,192},{96,208},{112... | collective-permute-start | bytes 98312
Sparse Core Ops, SparseCore 0:
  9.4 108.1 all-gather.1
where the time goes:
time: 341 us; the launch traced here: 340 us
  blocking collectives  128 us (38%)
  waiting for transfers between devices  114 us (33%)
  starting transfers between devices  71.7 us (21%)
  between operations  14.2 us (4%)
  matrix products  8.53 us (3%)
    unnamed x1, blocking collectives  128 us
    all_gather x1, waiting for transfers between devices, body(): lax.all_gather(masked_t2, 'ab', axis=0, tiled=True)  109 us
    unnamed x8, starting transfers between devices  71.7 us
    dot_general x1, matrix products, body(): jnp.dot(lax.all_gather(masked_t2, 'ab', axis=0, tiled=True), masked_v, pr...  8.53 us
  transfers between devices with their start and end apart: 9, of which 2 were waited for; matrix products, arithmetic and copies ran while one was open for 0% of the time, Pallas kernels for 0%

commit v1 on v0

v1 whole, which is shorter than its diff:
```python
import functools

import jax
import jax.numpy as jnp
from jax import lax
from jax.experimental import pallas as pl
from jax.experimental.pallas import tpu as pltpu
from jax.sharding import PartitionSpec as P

MESH = pl.DeviceIdType.MESH
CORES = 2
NX = 4
SUB = 8


def kernel(line, ny, nz, t_hbm, v_hbm, ij_ref, cd_ref, ab_ref, out_ref,
           tbuf, vraw, vhi, vlo, sbuf, xr, ys, yr, zs, zr, keep,
           t_sem, v_sem, line_recv, line_send, sib_recv, sib_send,
           x_recv, x_send, y_recv, y_send, z_recv, z_send):
    p, q = lax.axis_index("cd"), lax.axis_index("ab")
    x, y, h = p % NX, (p // NX) % ny, p // (NX * ny)
    core, i = q % CORES, q // CORES
    rows, depth = t_hbm.shape
    cols = v_hbm.shape[1]
    half = cols // 2
    subs = rows // SUB
    chunks = v_sem.shape[0]
    chunk = depth // chunks

    def plane(yy, xx):
        return (h * ny * NX + yy * NX + xx, q)

    sibling = (p, i * CORES + 1 - core)
    right, left = (p, q + CORES), (p, q - CORES)
    partner = ((p + ny * NX) % (nz * ny * NX), q)

    t_in = pltpu.make_async_copy(t_hbm, tbuf.at[q], t_sem)
    t_in.start()
    v_in = [pltpu.make_async_copy(v_hbm.at[pl.ds(c * chunk, chunk)], vraw.at[pl.ds(c * chunk, chunk)], v_sem.at[c])
            for c in range(chunks)]
    for copy in v_in:
        copy.start()

    barrier = pltpu.get_barrier_semaphore()

    def greet(device):
        pl.semaphore_signal(barrier, inc=1, device_id=device, device_id_type=MESH)

    greet(sibling)
    for d in range(1, NX):
        greet(plane(y, (x + d) % NX))
    for d in range(1, ny):
        greet(plane((y + d) % ny, x))
    if nz > 1:
        greet(partner)
    pl.when(i > 0)(lambda: greet(left))
    pl.when(i < line - 1)(lambda: greet(right))
    t_in.wait()

    sub = lax.broadcasted_iota(jnp.int32, (SUB, 128), 0)
    for g in range(subs):
        label = jnp.zeros((SUB, 128), jnp.int32)
        for r in range(SUB):
            label = jnp.where(sub == r, ij_ref[g * SUB + r], label)
        for c in range(0, depth, 128):
            block = tbuf[q, g * SUB:(g + 1) * SUB, c:c + 128]
            tbuf[q, g * SUB:(g + 1) * SUB, c:c + 128] = jnp.where(label == cd_ref[:, c:c + 128], block, 0.0)

    others = 1 + (NX - 1) + (ny - 1) + (1 if nz > 1 else 0)
    ends = jnp.where(i > 0, 1, 0) + jnp.where(i < line - 1, 1, 0)
    pl.semaphore_wait(barrier, others + ends)

    def line_copy(j, c, way, device):
        part = tbuf.at[j * CORES + core, pl.ds(c * SUB, SUB)]
        return pltpu.make_async_remote_copy(
            src_ref=part, dst_ref=part, send_sem=line_send.at[way, j, c], recv_sem=line_recv.at[j, c],
            device_id=device, device_id_type=MESH)

    def sib_copy(j, c):
        part = tbuf.at[j * CORES + core, pl.ds(c * SUB, SUB)]
        return pltpu.make_async_remote_copy(
            src_ref=part, dst_ref=part, send_sem=sib_send.at[j, c], recv_sem=sib_recv.at[j, c],
            device_id=sibling, device_id_type=MESH)

    def sib_wait(j, c):
        part = tbuf.at[j * CORES + 1 - core, pl.ds(c * SUB, SUB)]
        pltpu.make_async_remote_copy(
            src_ref=part, dst_ref=part, send_sem=sib_send.at[j, c], recv_sem=sib_recv.at[j, c],
            device_id=sibling, device_id_type=MESH).wait_recv()

    def forward(j, c, act):
        pl.when((j <= i) & (i < line - 1))(lambda: act(line_copy(j, c, 0, right)))
        pl.when((j >= i) & (i > 0))(lambda: act(line_copy(j, c, 1, left)))
        act(sib_copy(j, c))

    for c in range(subs):
        forward(i, c, lambda copy: copy.start())

    for c in range(chunks):
        v_in[c].wait()

        @pl.loop(0, chunk // 128)
        def _(b):
            start = pl.multiple_of(c * chunk + b * 128, 128)
            label = jnp.broadcast_to(cd_ref[:, pl.ds(start, 128)], (128, 128)).T
            for l in range(0, cols, 128):
                v = jnp.where(label == ab_ref[:, l:l + 128], vraw[pl.ds(start, 128), l:l + 128], 0.0)
                hi = v.astype(jnp.bfloat16)
                vhi[pl.ds(start, 128), l:l + 128] = hi
                vlo[pl.ds(start, 128), l:l + 128] = (v - hi.astype(jnp.float32)).astype(jnp.bfloat16)

    def x_copy(j, k, device):
        return pltpu.make_async_remote_copy(
            src_ref=sbuf.at[j, k], dst_ref=xr.at[j, x], send_sem=x_send.at[j, k], recv_sem=x_recv.at[j, x],
            device_id=device, device_id_type=MESH)

    def x_wait(j, k):
        pltpu.make_async_remote_copy(
            src_ref=sbuf.at[j, k], dst_ref=xr.at[j, k], send_sem=x_send.at[j, k], recv_sem=x_recv.at[j, k],
            device_id=plane(y, k), device_id_type=MESH).wait_recv()

    def y_copy(j):
        return pltpu.make_async_remote_copy(
            src_ref=ys.at[j], dst_ref=yr.at[j // ny, y], send_sem=y_send.at[j], recv_sem=y_recv.at[j // ny, y],
            device_id=plane(j % ny, x), device_id_type=MESH)

    def y_wait(hh, yy):
        pltpu.make_async_remote_copy(
            src_ref=ys.at[0], dst_ref=yr.at[hh, yy], send_sem=y_send.at[0], recv_sem=y_recv.at[hh, yy],
            device_id=plane(yy, x), device_id_type=MESH).wait_recv()

    def z_copy():
        return pltpu.make_async_remote_copy(
            src_ref=zs, dst_ref=zr, send_sem=z_send, recv_sem=z_recv, device_id=partner, device_id_type=MESH)

    low = lax.broadcasted_iota(jnp.int32, (8, half), 0) < 4

    def multiply(j):
        t = tbuf[pl.ds(j * CORES, CORES)].reshape(CORES * rows, depth)
        hi = t.astype(jnp.bfloat16)
        lo = (t - hi.astype(jnp.float32)).astype(jnp.bfloat16)
        a = jnp.dot(jnp.concatenate([hi, lo], axis=0), vhi[...], preferred_element_type=jnp.float32)
        b = jnp.dot(hi, vlo[...], preferred_element_type=jnp.float32)
        total = a[:CORES * rows] + a[CORES * rows:] + b
        for k in range(NX):
            base = (k // 2) * rows
            middle = total[base + 8:base + 16]
            turned = pltpu.roll(middle, 4, 0)
            if k % 2 == 0:
                full = total[base:base + 8]
                rest = jnp.where(low, middle[:, :half], turned[:, half:])
            else:
                full = total[base + 16:base + 24]
                rest = jnp.where(low, turned[:, :half], middle[:, half:])
            sbuf[j, k, :, :cols] = full
            sbuf[j, k, :, cols:] = rest
        for d in range(1, NX):
            k = (x + d) % NX
            x_copy(j, k, plane(y, k)).start()

    def reduce_x(j):
        for d in range(1, NX):
            x_wait(j, (x + d) % NX)
        mine = sbuf[j, x]
        for d in range(1, NX):
            mine = mine + xr[j, (x + d) % NX]
        ys[j] = mine
        pl.when(j % ny != y)(lambda: y_copy(j).start())

    def reduce_y(j):
        @pl.when(j % ny == y)
        def _():
            hh = j // ny
            for d in range(1, ny):
                y_wait(hh, (y + d) % ny)
            mine = ys[j]
            for d in range(1, ny):
                mine = mine + yr[hh, (y + d) % ny]

            @pl.when(hh == h)
            def _():
                keep[...] = mine

            @pl.when(hh != h)
            def _():
                zs[...] = mine
                z_copy().start()

    def let_go(j):
        for c in range(subs):
            forward(j, c, lambda copy: copy.wait_send())
        for d in range(1, NX):
            k = (x + d) % NX
            x_copy(j, k, plane(y, k)).wait_send()
        pl.when(j % ny != y)(lambda: y_copy(j).wait_send())

    def at(step, act):
        @pl.loop(0, 2)
        def _(side):
            j = i - step + side * 2 * step
            pl.when((j >= 0) & (j < line) & (step + 1 - side > 0))(lambda: act(j))

    @pl.loop(0, line + 2)
    def _(step):
        @pl.when(step < line)
        def _():
            @pl.when(step > 0)
            def _():
                @pl.loop(0, subs)
                def _(c):
                    def take(j):
                        line_copy(j, c, 0, right).wait_recv()
                        forward(j, c, lambda copy: copy.start())

                    pl.when(i - step >= 0)(lambda: take(i - step))
                    pl.when(i + step < line)(lambda: take(i + step))

            def ready(j):
                for c in range(subs):
                    sib_wait(j, c)
                multiply(j)

            at(step, ready)

        pl.when((step >= 1) & (step <= line))(lambda: at(step - 1, reduce_x))
        pl.when(step >= 2)(lambda: at(step - 2, reduce_y))

    if nz > 1:
        z_copy().wait_recv()
    mine = keep[...]
    if nz > 1:
        mine = mine + zr[...]
    full, rest = mine[:, :cols], mine[:, cols:]
    turned = pltpu.roll(rest, 4, 0)

    @pl.when(x % 2 == 0)
    def _():
        out_ref[:8] = full
        out_ref[8:12, :half] = rest[:4]
        out_ref[8:12, half:] = turned[:4]

    @pl.when(x % 2 == 1)
    def _():
        out_ref[:4, :half] = rest[:4]
        out_ref[:4, half:] = turned[:4]
        out_ref[4:12] = full

    @pl.loop(0, line)
    def _(j):
        let_go(j)
    if nz > 1:
        z_copy().wait_send()


def ladder(line, ny, nz, amplitudes, integrals, ij, cd, ab):
    rows, depth = amplitudes.shape
    cols = integrals.shape[1]
    subs = rows // SUB
    piece = (8, cols + cols // 2)
    dma = pltpu.SemaphoreType.DMA
    vmem = pl.BlockSpec(memory_space=pltpu.VMEM)
    chunks = min(4, depth // 128)
    return pl.pallas_call(
        functools.partial(kernel, line, ny, nz),
        out_shape=jax.ShapeDtypeStruct((rows // 2, cols), jnp.float32),
        in_specs=[pl.BlockSpec(memory_space=pltpu.HBM), pl.BlockSpec(memory_space=pltpu.HBM),
                  pl.BlockSpec(memory_space=pltpu.SMEM), vmem, vmem],
        out_specs=vmem,
        scratch_shapes=[
            pltpu.VMEM((line * CORES, rows, depth), jnp.float32),
            pltpu.VMEM((depth, cols), jnp.float32),
            pltpu.VMEM((depth, cols), jnp.bfloat16),
            pltpu.VMEM((depth, cols), jnp.bfloat16),
            pltpu.VMEM((line, NX) + piece, jnp.float32),
            pltpu.VMEM((line, NX) + piece, jnp.float32),
            pltpu.VMEM((line,) + piece, jnp.float32),
            pltpu.VMEM((nz, ny) + piece, jnp.float32),
            pltpu.VMEM(piece, jnp.float32),
            pltpu.VMEM(piece, jnp.float32),
            pltpu.VMEM(piece, jnp.float32),
            dma, dma((chunks,)),
            dma((line, subs)), dma((2, line, subs)),
            dma((line, subs)), dma((line, subs)),
            dma((line, NX)), dma((line, NX)),
            dma((nz, ny)), dma((line,)),
            dma, dma,
        ],
        compiler_params=pltpu.CompilerParams(
            collective_id=0, has_side_effects=True, vmem_limit_bytes=48 * 1024 * 1024),
    )(amplitudes, integrals, ij, cd.reshape(1, depth), ab.reshape(1, cols))


def solution(mesh):
    line = mesh.shape["ab"] // CORES
    planes = mesh.shape["cd"] // NX
    ny = min(4, planes)
    nz = planes // ny

    def body(amplitudes, integrals, residual_in, ij, cd, ab):
        return residual_in + ladder(line, ny, nz, amplitudes, integrals, ij, cd, ab)

    placed = (P("ab", "cd"), P("cd", "ab"), P("cd", "ab"), P("ab"), P("cd"), P("ab"))
    return jax.shard_map(body, mesh=mesh, in_specs=placed, out_specs=P("cd", "ab"), check_vma=False)
```

time: 341 us -> 69.4 us (0.20)
  the two profiles are of different devices: /device:TPU:20 before, /device:TPU:24 now
where the time goes in v1:
time: 69.4 us; the launch traced here: 69.1 us
  Pallas kernels  63.3 us (91%)
  local copies, waits for them, and re-layouts  5.15 us (7%)
    pallas_call x1, Pallas kernels, ladder(): pl.pallas_call(functools.partial(kernel, line, ny, nz), out_shape=jax.Sha...  63.3 us
    unnamed x12, local copies, waits for them, and re-layouts  5.15 us

profile of v1, /device:TPU:24, one launch (start us, length us, event | category | flops | bytes accessed | tf_op | source)
XLA Modules:
  0.0 69.1 jit_solution(5730522697033785742)
XLA Ops:
  0.0 0.0 copy-start
  0.0 2.2 %copy-done = f32[2048,512]{1,0:T(8,128)S(1)} copy-done((f32[2048,512]{1,0:T(8,128)S(1)}, f32[2048,512]{1,0:T(8,128)}, u32[]{:S(2)}) %copy-start) | copy-done | bytes 4194328
  2.2 0.0 copy-start.1
  2.2 0.9 %copy-done.1 = f32[24,2048]{1,0:T(8,128)S(1)} copy-done((f32[24,2048]{1,0:T(8,128)S(1)}, f32[24,2048]{1,0:T(8,128)}, u32[]{:S(2)}) %copy-start.1) | copy-done | bytes 196632
  3.1 0.0 copy-start.2
  3.1 0.7 %copy-done.2 = s32[2048]{0:T(1024)S(1)} copy-done((s32[2048]{0:T(1024)S(1)}, s32[2048]{0:T(1024)}, u32[]{:S(2)}) %copy-start.2) | copy-done | bytes 8216
  3.8 0.0 copy-start.3
  3.8 0.7 copy-done.3
  4.5 0.0 copy-start.4
  4.5 0.7 copy-done.4
  5.2 0.0 copy-start.5
  5.2 63.3 %shard_map.64 = f32[12,512]{1,0:T(8,128)S(1)} custom-call(f32[24,2048]{1,0:T(8,128)S(1)} %copy-done.1, f32[2048,512]{1,0:T(8,128)S(1)} %copy-done, s32[24]{0:T(128)S(1)} %copy-done.4, s32[1,2048]{1,0:T(1,128)S(1)} %bitcast.2, s32[1,512]{1,0:T(1,128)S(1)} %bitcast.3), custom_call_target="tpu_custom_call" | custom-call | tf_op jit(solution)/shard_map/pallas_call | solution.py:263
  68.4 0.0 copy-done.5
  68.5 0.6 add.3
Async XLA Ops:
  0.0 2.2 %copy-start = (f32[2048,512]{1,0:T(8,128)S(1)}, f32[2048,512]{1,0:T(8,128)}, u32[]{:S(2)}) copy-start(f32[2048,512]{1,0:T(8,128)} %v_hbm.1) | copy-start | bytes 12582916
  2.2 0.9 %copy-start.1 = (f32[24,2048]{1,0:T(8,128)S(1)}, f32[24,2048]{1,0:T(8,128)}, u32[]{:S(2)}) copy-start(f32[24,2048]{1,0:T(8,128)} %t_hbm.1) | copy-start | bytes 589828
  3.1 0.7 %copy-start.2 = (s32[2048]{0:T(1024)S(1)}, s32[2048]{0:T(1024)}, u32[]{:S(2)}) copy-start(s32[2048]{0:T(1024)} %param.10) | copy-start | bytes 24580
  3.8 0.7 copy-start.3
  4.5 0.7 copy-start.4
  5.2 63.3 %copy-start.5 = (f32[12,512]{1,0:T(8,128)S(1)}, f32[12,512]{1,0:T(8,128)}, u32[]{:S(2)}) copy-start(f32[12,512]{1,0:T(8,128)} %param.8) | copy-start | bytes 73732

commit v2 on v1

v2 whole, which is shorter than its diff:
```python
import functools

import jax
import jax.numpy as jnp
from jax import lax
from jax.experimental import pallas as pl
from jax.experimental.pallas import tpu as pltpu
from jax.sharding import PartitionSpec as P

MESH = pl.DeviceIdType.MESH
CORES = 2
NX = 4
NY = 4
SUB = 8
CUTS = 2
PARTS = 4
FIRST = 4


def kernel(line, ny, nz, t_hbm, v_hbm, res_hbm, ij_hbm, cd_hbm, ab_hbm, out_ref,
           tbuf, vraw, vhi, vlo, acc, sbuf, xr, ys, yr, zs, zr, keep, res, ij_ref, cd_ref, ab_ref,
           t_sem, v_sem, small_sem, line_recv, line_send, sib_recv, sib_send,
           x_recv, x_send, y_recv, y_send, z_recv, z_send, z_here):
    p, q = lax.axis_index("cd"), lax.axis_index("ab")
    x, y, h = p % NX, (p // NX) % ny, p // (NX * ny)
    core, i = q % CORES, q // CORES
    rows, depth = t_hbm.shape
    cols = v_hbm.shape[1]
    half = cols // 2
    subs = rows // SUB * CUTS
    width = depth // CUTS
    chunks = v_sem.shape[0]
    chunk = depth // chunks

    def plane(yy, xx):
        return (h * ny * NX + yy * NX + xx, q)

    sibling = (p, i * CORES + 1 - core)
    right, left = (p, q + CORES), (p, q - CORES)
    partner = ((p + ny * NX) % (nz * ny * NX), q)

    t_in = pltpu.make_async_copy(t_hbm, tbuf.at[q], t_sem)
    t_in.start()

    barrier = pltpu.get_barrier_semaphore()

    def greet(device):
        pl.semaphore_signal(barrier, inc=1, device_id=device, device_id_type=MESH)

    if nz > 1:
        pl.when(h == 0)(lambda: greet(partner))
    pl.when(i > 0)(lambda: greet(left))
    pl.when(i < line - 1)(lambda: greet(right))
    for d in range(1, NX):
        greet(plane(y, (x + d) % NX))
    for d in range(1, ny):
        greet(plane((y + d) % ny, x))
    greet(sibling)

    small = [pltpu.make_async_copy(a, b, small_sem.at[n])
             for n, (a, b) in enumerate(((ij_hbm, ij_ref), (cd_hbm, cd_ref), (ab_hbm, ab_ref), (res_hbm, res)))]
    for copy in small:
        copy.start()
    v_in = [pltpu.make_async_copy(v_hbm.at[pl.ds(c * chunk, chunk)], vraw.at[pl.ds(c * chunk, chunk)], v_sem.at[c])
            for c in range(chunks)]
    for copy in v_in:
        copy.start()

    small[0].wait()
    small[1].wait()
    t_in.wait()
    sub = lax.broadcasted_iota(jnp.int32, (SUB, 128), 0)
    for g in range(rows // SUB):
        label = jnp.zeros((SUB, 128), jnp.int32)
        for r in range(SUB):
            label = jnp.where(sub == r, ij_ref[g * SUB + r], label)
        for c in range(0, depth, 128):
            block = tbuf[q, g * SUB:(g + 1) * SUB, c:c + 128]
            tbuf[q, g * SUB:(g + 1) * SUB, c:c + 128] = jnp.where(label == cd_ref[:, c:c + 128], block, 0.0)

    others = 1 + (NX - 1) + (ny - 1) + (jnp.where(h > 0, 1, 0) if nz > 1 else 0)
    ends = jnp.where(i > 0, 1, 0) + jnp.where(i < line - 1, 1, 0)
    pl.semaphore_wait(barrier, others + ends)

    def remote(src, dst, send, recv, device):
        return pltpu.make_async_remote_copy(
            src_ref=src, dst_ref=dst, send_sem=send, recv_sem=recv, device_id=device, device_id_type=MESH)

    def piece(j, which, c):
        start = pl.multiple_of(c % CUTS * width, width)
        return tbuf.at[j * CORES + which, pl.ds(pl.multiple_of(c // CUTS * SUB, SUB), SUB), pl.ds(start, width)]

    m = line // 2

    def behind(side):
        return jnp.where(side == 0, i, line - 1 - i)

    def number(side, b):
        return jnp.where(side == 0, b, line - 1 - b)

    def late(side):
        return (h == 1 - side) if nz > 1 else h < 0

    def near(side):
        return jnp.where(late(side), jnp.maximum(behind(side) - m, 0), 0)

    def arrival(side, n):
        k = near(side)
        r = n - k * FIRST
        t = r - m * subs
        rest = subs - FIRST
        b = jnp.where(k == 0, behind(side) - 1 - n // subs, m - 1 - r // subs)
        c = jnp.where(k == 0, n % subs, r % subs)
        before, after = (k > 0) & (r < 0), (k > 0) & (t >= 0)
        b = jnp.where(before, behind(side) - 1 - n // FIRST, jnp.where(after, m + t // rest, b))
        c = jnp.where(before, n % FIRST, jnp.where(after, FIRST + t % rest, c))
        return number(side, b), c

    def withheld(side):
        return late(side) & (behind(side) >= m) & (behind(side) < line - 1)

    def line_copy(j, c, way):
        part = piece(j, core, c)
        return remote(part, part, line_send.at[way, j], line_recv.at[j, c], right if way == 0 else left)

    def sib_copy(j, c):
        part = piece(j, core, c)
        return remote(part, part, sib_send.at[j], sib_recv.at[j], sibling)

    def forward(j, c, way):
        pl.when(i < line - 1 if way == 0 else i > 0)(lambda: line_copy(j, c, way).start())

    def forward_done(j):
        mine = tbuf.at[j * CORES + core]
        for way, there in ((0, (j <= i) & (i < line - 1)), (1, (j >= i) & (i > 0))):
            @pl.when(there & ((j != i) | jnp.logical_not(withheld(way))))
            def _():
                remote(mine, mine, line_send.at[way, j], line_recv.at[j, 0], sibling).wait_send()
        remote(mine, mine, sib_send.at[j], sib_recv.at[j], sibling).wait_send()

    def sib_wait(j):
        other = tbuf.at[j * CORES + 1 - core]
        remote(other, other, sib_send.at[j], sib_recv.at[j], sibling).wait_recv()

    for c in range(subs):
        for way in range(2):
            if c < FIRST:
                forward(i, c, way)
            else:
                pl.when(jnp.logical_not(withheld(way)))(lambda: forward(i, c, way))
    for c in range(subs):
        sib_copy(i, c).start()

    if nz > 1:
        @pl.when(h > 0)
        def _():
            pl.semaphore_signal(z_here, inc=1, device_id=partner, device_id_type=MESH)

    small[2].wait()
    for c in range(chunks):
        v_in[c].wait()

        @pl.loop(0, chunk // 128)
        def _(b):
            start = pl.multiple_of(c * chunk + b * 128, 128)
            label = jnp.broadcast_to(cd_ref[:, pl.ds(start, 128)], (128, 128)).T
            for l in range(0, cols, 128):
                v = jnp.where(label == ab_ref[:, l:l + 128], vraw[pl.ds(start, 128), l:l + 128], 0.0)
                hi = v.astype(jnp.bfloat16)
                vhi[pl.ds(start, 128), l:l + 128] = hi
                vlo[pl.ds(start, 128), l:l + 128] = (v - hi.astype(jnp.float32)).astype(jnp.bfloat16)

    def x_copy(j, d):
        k = (x + d) % NX
        return remote(sbuf.at[j, k], xr.at[j, d - 1], x_send.at[j], x_recv.at[j], plane(y, k))

    def y_copy(j):
        d = (j - y + ny) % ny
        return remote(ys.at[j], yr.at[j // ny, d - 1], y_send.at[j], y_recv.at[j // ny], plane(j % ny, x))

    def z_copy():
        return remote(zs, zr, z_send, z_recv, partner)

    low = lax.broadcasted_iota(jnp.int32, (8, half), 0) < 4

    def product(blocks, start, size):
        t = jnp.concatenate([tbuf[pl.ds(j * CORES, CORES), :, pl.ds(start, size)].reshape(CORES * rows, size)
                             for j in blocks], axis=0)
        n = t.shape[0]
        hi = t.astype(jnp.bfloat16)
        lo = (t - hi.astype(jnp.float32)).astype(jnp.bfloat16)
        a = jnp.dot(jnp.concatenate([hi, lo], axis=0), vhi[pl.ds(start, size)], preferred_element_type=jnp.float32)
        b = jnp.dot(hi, vlo[pl.ds(start, size)], preferred_element_type=jnp.float32)
        return a[:n] + a[n:] + b

    def hand_out(j, n):
        for k in range(NX):
            base = (k // 2) * rows
            middle = acc[n, base + 8:base + 16]
            turned = pltpu.roll(middle, 4, 0)
            if k % 2 == 0:
                full = acc[n, base:base + 8]
                rest = jnp.where(low, middle[:, :half], turned[:, half:])
            else:
                full = acc[n, base + 16:base + 24]
                rest = jnp.where(low, turned[:, :half], middle[:, half:])
            sbuf[j, k, :, :cols] = full
            sbuf[j, k, :, cols:] = rest
        for d in range(1, NX):
            x_copy(j, d).start()

    def reduce_x(j):
        remote(xr.at[j], xr.at[j], x_send.at[j], x_recv.at[j], sibling).wait_recv()
        mine = sbuf[j, x]
        for d in range(1, NX):
            mine = mine + xr[j, d - 1]
        ys[j] = mine
        pl.when(j % ny != y)(lambda: y_copy(j).start())

    def reduce_y(j):
        @pl.when(j % ny == y)
        def _():
            hh = j // ny
            mine = ys[j]
            if ny > 1:
                remote(yr.at[hh], yr.at[hh], y_send.at[j], y_recv.at[hh], sibling).wait_recv()
                for d in range(1, ny):
                    mine = mine + yr[hh, d - 1]

            @pl.when(hh == h)
            def _():
                keep[...] = mine

            @pl.when(hh != h)
            def _():
                zs[...] = mine
                pl.when(h == 0)(lambda: pl.semaphore_wait(z_here, 1))
                z_copy().start()

    def let_go(j):
        forward_done(j)
        sent = sbuf.at[j, pl.ds(0, NX - 1)]
        remote(sent, sent, x_send.at[j], x_recv.at[j], sibling).wait_send()
        pl.when(j % ny != y)(lambda: y_copy(j).wait_send())

    def complete(side, step):
        u, k = behind(side), near(side)
        b = jnp.where(k > 0, m + (k * FIRST + subs - 1) // subs, u) - step
        there = jnp.where(step == 0, side == 0, (step > 0) & (b >= 0) & (b < jnp.where(k > 0, m, u)))
        return there, jnp.where(step == 0, i, number(side, b))

    def rest(side, step, act):
        @pl.when(step == behind(side))
        def _():
            @pl.loop(0, near(side))
            def _(n):
                act(number(side, m + n))

    def at(step, act):
        @pl.loop(0, 2)
        def _(side):
            there, j = complete(side, step)
            pl.when(there)(lambda: act(j))
            rest(side, step, act)

    def whole(j):
        sib_wait(j)
        acc[0] = product([j], 0, depth)
        hand_out(j, 0)

    def both(step, part):
        (there, j), (there_too, j_too) = complete(0, step), complete(1, step)

        @pl.when(there | there_too)
        def _():
            @pl.when(part == 0)
            def _():
                pl.when(there)(lambda: sib_wait(j))
                pl.when(there_too)(lambda: sib_wait(j_too))

            size = depth // PARTS
            start = pl.multiple_of(part * size, size)
            term = product([jnp.where(there, j, j_too), jnp.where(there_too, j_too, j)], start, size)
            term = term.reshape(2, CORES * rows, cols)

            @pl.when(part == 0)
            def _():
                acc[...] = term

            @pl.when(part > 0)
            def _():
                acc[...] += term

            @pl.when(part == PARTS - 1)
            def _():
                pl.when(there)(lambda: hand_out(j, 0))
                pl.when(there_too)(lambda: hand_out(j_too, 1))

        @pl.when(part == PARTS - 1)
        def _():
            @pl.loop(0, 2)
            def _(side):
                rest(side, step, whole)

    end = (i == 0) | (i == line - 1)

    @pl.loop(0, line + 2)
    def _(step):
        @pl.loop(0, subs)
        def _(c):
            for side in range(2):
                @pl.when((step > 0) & (step <= behind(side)))
                def _():
                    j, piece_number = arrival(side, (step - 1) * subs + c)
                    line_copy(j, piece_number, side).wait_recv()
                    forward(j, piece_number, side)
                    sib_copy(j, piece_number).start()

            @pl.when(jnp.logical_not(end) & (c < PARTS))
            def _():
                both(step - 1, c)

        for side in range(2):
            @pl.when(withheld(side) & (step == behind(side)))
            def _():
                for c in range(FIRST, subs):
                    forward(i, c, side)

        pl.when(end)(lambda: at(step, whole))

        done = jnp.where(end, step, step - 1)
        at(done - 1, reduce_x)
        at(done - 2, reduce_y)
        at(done - 2, let_go)

    small[3].wait()
    if nz > 1:
        z_copy().wait_recv()
    mine = keep[...]
    if nz > 1:
        mine = mine + zr[...]
    full, rest = mine[:, :cols], mine[:, cols:]
    turned = pltpu.roll(rest, 4, 0)

    @pl.when(x % 2 == 0)
    def _():
        out_ref[:8] = full + res[:8]
        out_ref[8:12, :half] = rest[:4] + res[8:12, :half]
        out_ref[8:12, half:] = turned[:4] + res[8:12, half:]

    @pl.when(x % 2 == 1)
    def _():
        out_ref[:4, :half] = rest[:4] + res[:4, :half]
        out_ref[:4, half:] = turned[:4] + res[:4, half:]
        out_ref[4:12] = full + res[4:12]

    if nz > 1:
        z_copy().wait_send()
    for way in range(2):
        @pl.when(withheld(way))
        def _():
            mine = tbuf.at[i * CORES + core]
            remote(mine, mine, line_send.at[way, i], line_recv.at[i, 0], sibling).wait_send()


def ladder(line, ny, nz, amplitudes, integrals, residual, ij, cd, ab):
    rows, depth = amplitudes.shape
    cols = integrals.shape[1]
    subs = rows // SUB * CUTS
    piece = (8, cols + cols // 2)
    dma = pltpu.SemaphoreType.DMA
    chunks = min(4, depth // 128)
    return pl.pallas_call(
        functools.partial(kernel, line, ny, nz),
        out_shape=jax.ShapeDtypeStruct((rows // 2, cols), jnp.float32),
        in_specs=[pl.BlockSpec(memory_space=pltpu.HBM)] * 6,
        out_specs=pl.BlockSpec(memory_space=pltpu.VMEM),
        scratch_shapes=[
            pltpu.VMEM((line * CORES, rows, depth), jnp.float32),
            pltpu.VMEM((depth, cols), jnp.float32),
            pltpu.VMEM((depth, cols), jnp.bfloat16),
            pltpu.VMEM((depth, cols), jnp.bfloat16),
            pltpu.VMEM((2, CORES * rows, cols), jnp.float32),
            pltpu.VMEM((line, NX) + piece, jnp.float32),
            pltpu.VMEM((line, NX - 1) + piece, jnp.float32),
            pltpu.VMEM((line,) + piece, jnp.float32),
            pltpu.VMEM((nz, max(1, ny - 1)) + piece, jnp.float32),
            pltpu.VMEM(piece, jnp.float32),
            pltpu.VMEM(piece, jnp.float32),
            pltpu.VMEM(piece, jnp.float32),
            pltpu.VMEM((rows // 2, cols), jnp.float32),
            pltpu.SMEM((rows,), jnp.int32),
            pltpu.VMEM((1, depth), jnp.int32),
            pltpu.VMEM((1, cols), jnp.int32),
            dma, dma((chunks,)), dma((4,)),
            dma((line, subs)), dma((2, line)),
            dma((line,)), dma((line,)),
            dma((line,)), dma((line,)),
            dma((nz,)), dma((line,)),
            dma, dma, pltpu.SemaphoreType.REGULAR,
        ],
        compiler_params=pltpu.CompilerParams(
            collective_id=0, has_side_effects=True, vmem_limit_bytes=63 * 1024 * 1024),
    )(amplitudes, integrals, residual, ij, cd.reshape(1, depth), ab.reshape(1, cols))


def solution(mesh):
    line = mesh.shape["ab"] // CORES
    planes = mesh.shape["cd"] // NX
    ny = min(NY, planes)
    nz = planes // ny

    placed = (P("ab", "cd"), P("cd", "ab"), P("cd", "ab"), P("ab"), P("cd"), P("ab"))
    return jax.shard_map(functools.partial(ladder, line, ny, nz), mesh=mesh, in_specs=placed,
                         out_specs=P("cd", "ab"), check_vma=False)
```

time: 69.4 us -> 59 us (0.85)
  the two profiles are of different devices: /device:TPU:24 before, /device:TPU:224 now
where the time goes in v2:
time: 59 us; the launch traced here: 58.9 us
  Pallas kernels  57.5 us (97%)
  local copies, waits for them, and re-layouts  1.38 us (2%)
    pallas_call x1, Pallas kernels, ladder(): pl.pallas_call(functools.partial(kernel, line, ny, nz), out_shape=jax.Sha...  57.5 us
    unnamed x1, local copies, waits for them, and re-layouts  1.38 us

profile of v2, /device:TPU:224, one launch (start us, length us, event | category | flops | bytes accessed | tf_op | source)
XLA Modules:
  0.0 58.9 jit_solution(146289096821686884)
XLA Ops:
  0.0 57.5 %shard_map.64 = f32[12,512]{1,0:T(8,128)} custom-call(f32[24,2048]{1,0:T(8,128)} %t_hbm.1, f32[2048,512]{1,0:T(8,128)} %v_hbm.1, f32[12,512]{1,0:T(8,128)} %res_hbm.1, s32[24]{0:T(128)} %ij_hbm.1, s32[1,2048]{1,0:T(1,128)} %bitcast.2, s32[1,512]{1,0:T(1,128)} %bitcast.3), custom_call_target="tpu_custom_call" | custom-call | tf_op jit(solution)/shard_map/pallas_call | solution.py:373
  57.5 1.4 %copy.8 = f32[12,512]{1,0:T(8,128)} copy(f32[12,512]{1,0:T(8,128)} %shard_map.64) | data formatting | bytes 49152

commit v3 on v2

--- a/solution.py
+++ b/solution.py
@@ -91,6 +91,7 @@
         return tbuf.at[j * CORES + which, pl.ds(pl.multiple_of(c // CUTS * SUB, SUB), SUB), pl.ds(start, width)]
 
     m = line // 2
+    held = subs - FIRST
 
     def behind(side):
         return jnp.where(side == 0, i, line - 1 - i)
@@ -99,25 +100,32 @@
         return jnp.where(side == 0, b, line - 1 - b)
 
     def late(side):
-        return (h == 1 - side) if nz > 1 else h < 0
+        return (h > 0) & (side == 0)
 
     def near(side):
         return jnp.where(late(side), jnp.maximum(behind(side) - m, 0), 0)
 
     def arrival(side, n):
         k = near(side)
-        r = n - k * FIRST
-        t = r - m * subs
-        rest = subs - FIRST
-        b = jnp.where(k == 0, behind(side) - 1 - n // subs, m - 1 - r // subs)
-        c = jnp.where(k == 0, n % subs, r % subs)
-        before, after = (k > 0) & (r < 0), (k > 0) & (t >= 0)
-        b = jnp.where(before, behind(side) - 1 - n // FIRST, jnp.where(after, m + t // rest, b))
-        c = jnp.where(before, n % FIRST, jnp.where(after, FIRST + t % rest, c))
-        return number(side, b), c
+        ahead = k * FIRST
+        r = n - ahead
+        far = (k > 0) & (r >= 0) & (r < m * subs)
+        e = jnp.where((k > 0) & (r >= m * subs), n - m * subs, n)
+        b = jnp.where(far, m - 1 - r // subs, behind(side) - 1 - e // subs)
+        c = jnp.where(far, r % subs, e % subs)
+        return number(side, b), c, (k == 0) | (r < -held) | (r >= 0)
+
+    def keeps(side):
+        return late(side) & (behind(side) >= m) & (behind(side) < line - 1)
+
+    def kept(side, n):
+        k = near(side)
+        r = jnp.where(k > 0, k * FIRST - held + n, n)
+        return (number(side, jnp.where(k > 0, behind(side) - 1 - r // subs, m)),
+                jnp.where(k > 0, r % subs, FIRST + n))
 
     def withheld(side):
-        return late(side) & (behind(side) >= m) & (behind(side) < line - 1)
+        return keeps(side) & (near(side) == 0)
 
     def line_copy(j, c, way):
         part = piece(j, core, c)
@@ -245,28 +253,22 @@
 
     def complete(side, step):
         u, k = behind(side), near(side)
-        b = jnp.where(k > 0, m + (k * FIRST + subs - 1) // subs, u) - step
-        there = jnp.where(step == 0, side == 0, (step > 0) & (b >= 0) & (b < jnp.where(k > 0, m, u)))
-        return there, jnp.where(step == 0, i, number(side, b))
-
-    def rest(side, step, act):
-        @pl.when(step == behind(side))
-        def _():
-            @pl.loop(0, near(side))
-            def _(n):
-                act(number(side, m + n))
+        early, lead = k * FIRST // subs, (k * FIRST + subs - 1) // subs
+        far = (k > 0) & (step > early)
+        b = jnp.where(far, m + lead, u) - step
+        there = (step > 0) & (b >= jnp.where(k > 0, 1, 0)) & (jnp.logical_not(far) | (b < m))
+        return jnp.where(step == 0, side == 0, there), jnp.where(step == 0, i, number(side, b))
 
     def at(step, act):
         @pl.loop(0, 2)
         def _(side):
             there, j = complete(side, step)
             pl.when(there)(lambda: act(j))
-            rest(side, step, act)
 
     def whole(j):
         sib_wait(j)
-        acc[0] = product([j], 0, depth)
-        hand_out(j, 0)
+        acc[2] = product([j], 0, depth)
+        hand_out(j, 2)
 
     def both(step, part):
         (there, j), (there_too, j_too) = complete(0, step), complete(1, step)
@@ -285,22 +287,19 @@
 
             @pl.when(part == 0)
             def _():
-                acc[...] = term
+                acc[:2] = term
 
             @pl.when(part > 0)
             def _():
-                acc[...] += term
+                acc[:2] += term
 
             @pl.when(part == PARTS - 1)
             def _():
                 pl.when(there)(lambda: hand_out(j, 0))
                 pl.when(there_too)(lambda: hand_out(j_too, 1))
 
-        @pl.when(part == PARTS - 1)
-        def _():
-            @pl.loop(0, 2)
-            def _(side):
-                rest(side, step, whole)
+    u, k = behind(0), near(0)
+    last_far, rest = 0, m
 
     end = (i == 0) | (i == line - 1)
 
@@ -311,26 +310,49 @@
             for side in range(2):
                 @pl.when((step > 0) & (step <= behind(side)))
                 def _():
-                    j, piece_number = arrival(side, (step - 1) * subs + c)
-                    line_copy(j, piece_number, side).wait_recv()
-                    forward(j, piece_number, side)
-                    sib_copy(j, piece_number).start()
+                    n = (step - 1) * subs + c
+                    j, number_in_block, on = arrival(side, n)
+                    line_copy(j, number_in_block, side).wait_recv()
+                    pl.when(on)(lambda: forward(j, number_in_block, side))
+
+                    @pl.when(keeps(side) & (n == near(side) * FIRST + m * subs - 1))
+                    def _():
+                        for e in range(held):
+                            forward(*kept(side, e), side)
+
+                    sib_copy(j, number_in_block).start()
+
+            pl.when((k > 0) & ((step - 1) * subs + c == k * FIRST + m * subs - 1))(lambda: whole(last_far))
 
             @pl.when(jnp.logical_not(end) & (c < PARTS))
             def _():
                 both(step - 1, c)
 
-        for side in range(2):
-            @pl.when(withheld(side) & (step == behind(side)))
-            def _():
-                for c in range(FIRST, subs):
-                    forward(i, c, side)
-
         pl.when(end)(lambda: at(step, whole))
-
         done = jnp.where(end, step, step - 1)
-        at(done - 1, reduce_x)
-        at(done - 2, reduce_y)
+        final = jnp.where(end, u - 1, u)
+
+        @pl.when((k == 0) | (step <= final))
+        def _():
+            at(done - 1, reduce_x)
+            at(done - 2, reduce_y)
+
+        @pl.when((k > 0) & (step == final))
+        def _():
+            pl.when(jnp.logical_not(end))(lambda: at(done, reduce_x))
+            reduce_x(last_far)
+            at(done - 1, reduce_y)
+            pl.when(jnp.logical_not(end))(lambda: at(done, reduce_y))
+
+        @pl.when((k > 0) & (step == u))
+        def _():
+            whole(rest)
+            reduce_y(last_far)
+            reduce_x(rest)
+            reduce_y(rest)
+            let_go(last_far)
+            let_go(rest)
+
         at(done - 2, let_go)
 
     small[3].wait()
@@ -380,7 +402,7 @@
             pltpu.VMEM((depth, cols), jnp.float32),
             pltpu.VMEM((depth, cols), jnp.bfloat16),
             pltpu.VMEM((depth, cols), jnp.bfloat16),
-            pltpu.VMEM((2, CORES * rows, cols), jnp.float32),
+            pltpu.VMEM((3, CORES * rows, cols), jnp.float32),
             pltpu.VMEM((line, NX) + piece, jnp.float32),
             pltpu.VMEM((line, NX - 1) + piece, jnp.float32),
             pltpu.VMEM((line,) + piece, jnp.float32),

time: 59 us -> 57.2 us (0.969)
  Pallas kernels: 57.5 us -> 55.6 us
    pallas_call x1, Pallas kernels: 57.5 us -> 55.6 us  [ladder(): pl.pallas_call(functools.partial(kernel, line, ny, nz), out_shape=jax.Sha...]
where the time goes in v3:
time: 57.2 us; the launch traced here: 57 us
  Pallas kernels  55.6 us (97%)
  local copies, waits for them, and re-layouts  1.38 us (2%)
    pallas_call x1, Pallas kernels, ladder(): pl.pallas_call(functools.partial(kernel, line, ny, nz), out_shape=jax.Sha...  55.6 us
    unnamed x1, local copies, waits for them, and re-layouts  1.38 us

profile of v3, /device:TPU:224, one launch (start us, length us, event | category | flops | bytes accessed | tf_op | source)
XLA Modules:
  0.0 57.0 jit_solution(17619326135125824292)
XLA Ops:
  0.0 55.6 %shard_map.64 = f32[12,512]{1,0:T(8,128)} custom-call(f32[24,2048]{1,0:T(8,128)} %t_hbm.1, f32[2048,512]{1,0:T(8,128)} %v_hbm.1, f32[12,512]{1,0:T(8,128)} %res_hbm.1, s32[24]{0:T(128)} %ij_hbm.1, s32[1,2048]{1,0:T(1,128)} %bitcast.2, s32[1,512]{1,0:T(1,128)} %bitcast.3), custom_call_target="tpu_custom_call" | custom-call | tf_op jit(solution)/shard_map/pallas_call | solution.py:395
  55.6 1.4 %copy.8 = f32[12,512]{1,0:T(8,128)} copy(f32[12,512]{1,0:T(8,128)} %shard_map.64) | data formatting | bytes 49152

commit v4 on v3

--- a/solution.py
+++ b/solution.py
@@ -225,6 +225,13 @@
         ys[j] = mine
         pl.when(j % ny != y)(lambda: y_copy(j).start())
 
+    def send_z():
+        pl.when(h == 0)(lambda: pl.semaphore_wait(z_here, 1))
+        z_copy().start()
+
+    patient = ((h > 0) & (i <= m)) | ((h == 0) & (i == line - 1)) if nz > 1 else False
+    halfway = patient & (i < 2)
+
     def reduce_y(j):
         @pl.when(j % ny == y)
         def _():
@@ -242,8 +249,7 @@
             @pl.when(hh != h)
             def _():
                 zs[...] = mine
-                pl.when(h == 0)(lambda: pl.semaphore_wait(z_here, 1))
-                z_copy().start()
+                pl.when(jnp.logical_not(patient))(send_z)
 
     def let_go(j):
         forward_done(j)
@@ -354,9 +360,11 @@
             let_go(rest)
 
         at(done - 2, let_go)
+        pl.when(halfway & (step == line - 2))(send_z)
 
     small[3].wait()
     if nz > 1:
+        pl.when(patient & jnp.logical_not(halfway))(send_z)
         z_copy().wait_recv()
     mine = keep[...]
     if nz > 1:

time: 57.2 us -> 55.6 us (0.972)
  Pallas kernels: 55.6 us -> 54 us
    pallas_call x1, Pallas kernels: 55.6 us -> 54 us  [ladder(): pl.pallas_call(functools.partial(kernel, line, ny, nz), out_shape=jax.Sha...]
where the time goes in v4:
time: 55.6 us; the launch traced here: 55.4 us
  Pallas kernels  54 us (97%)
  local copies, waits for them, and re-layouts  1.38 us (2%)
    pallas_call x1, Pallas kernels, ladder(): pl.pallas_call(functools.partial(kernel, line, ny, nz), out_shape=jax.Sha...  54 us
    unnamed x1, local copies, waits for them, and re-layouts  1.38 us

profile of v4, /device:TPU:224, one launch (start us, length us, event | category | flops | bytes accessed | tf_op | source)
XLA Modules:
  0.0 55.4 jit_solution(10588497191704558824)
XLA Ops:
  0.0 54.0 %shard_map.64 = f32[12,512]{1,0:T(8,128)} custom-call(f32[24,2048]{1,0:T(8,128)} %t_hbm.1, f32[2048,512]{1,0:T(8,128)} %v_hbm.1, f32[12,512]{1,0:T(8,128)} %res_hbm.1, s32[24]{0:T(128)} %ij_hbm.1, s32[1,2048]{1,0:T(1,128)} %bitcast.2, s32[1,512]{1,0:T(1,128)} %bitcast.3), custom_call_target="tpu_custom_call" | custom-call | tf_op jit(solution)/shard_map/pallas_call | solution.py:403
  54.0 1.4 %copy.8 = f32[12,512]{1,0:T(8,128)} copy(f32[12,512]{1,0:T(8,128)} %shard_map.64) | data formatting | bytes 49152

commit v5 on v4

--- a/solution.py
+++ b/solution.py
@@ -131,8 +131,8 @@
         part = piece(j, core, c)
         return remote(part, part, line_send.at[way, j], line_recv.at[j, c], right if way == 0 else left)
 
-    def sib_copy(j, c):
-        part = piece(j, core, c)
+    def sib_copy(j, g):
+        part = tbuf.at[j * CORES + core, pl.ds(pl.multiple_of(g * SUB, SUB), SUB)]
         return remote(part, part, sib_send.at[j], sib_recv.at[j], sibling)
 
     def forward(j, c, way):
@@ -156,8 +156,8 @@
                 forward(i, c, way)
             else:
                 pl.when(jnp.logical_not(withheld(way)))(lambda: forward(i, c, way))
-    for c in range(subs):
-        sib_copy(i, c).start()
+    for g in range(rows // SUB):
+        sib_copy(i, g).start()
 
     if nz > 1:
         @pl.when(h > 0)
@@ -214,7 +214,7 @@
                 rest = jnp.where(low, turned[:, :half], middle[:, half:])
             sbuf[j, k, :, :cols] = full
             sbuf[j, k, :, cols:] = rest
-        for d in range(1, NX):
+        for d in sorted(range(1, NX), key=lambda d: -min(d, NX - d)):
             x_copy(j, d).start()
 
     def reduce_x(j):
@@ -326,7 +326,8 @@
                         for e in range(held):
                             forward(*kept(side, e), side)
 
-                    sib_copy(j, number_in_block).start()
+                    pl.when(number_in_block % CUTS == CUTS - 1)(
+                        lambda: sib_copy(j, number_in_block // CUTS).start())
 
             pl.when((k > 0) & ((step - 1) * subs + c == k * FIRST + m * subs - 1))(lambda: whole(last_far))
 

time: 55.6 us -> 55.3 us (level)
  no operation moved by 1% of the time
where the time goes in v5:
time: 55.3 us; the launch traced here: 55.2 us
  Pallas kernels  53.8 us (97%)
  local copies, waits for them, and re-layouts  1.38 us (2%)
    pallas_call x1, Pallas kernels, ladder(): pl.pallas_call(functools.partial(kernel, line, ny, nz), out_shape=jax.Sha...  53.8 us
    unnamed x1, local copies, waits for them, and re-layouts  1.38 us

profile of v5, /device:TPU:224, one launch (start us, length us, event | category | flops | bytes accessed | tf_op | source)
XLA Modules:
  0.0 55.2 jit_solution(10985043160512332529)
XLA Ops:
  0.0 53.8 %shard_map.64 = f32[12,512]{1,0:T(8,128)} custom-call(f32[24,2048]{1,0:T(8,128)} %t_hbm.1, f32[2048,512]{1,0:T(8,128)} %v_hbm.1, f32[12,512]{1,0:T(8,128)} %res_hbm.1, s32[24]{0:T(128)} %ij_hbm.1, s32[1,2048]{1,0:T(1,128)} %bitcast.2, s32[1,512]{1,0:T(1,128)} %bitcast.3), custom_call_target="tpu_custom_call" | custom-call | tf_op jit(solution)/shard_map/pallas_call | solution.py:404
  53.8 1.4 %copy.8 = f32[12,512]{1,0:T(8,128)} copy(f32[12,512]{1,0:T(8,128)} %shard_map.64) | data formatting | bytes 49152

commit v6 on v5

--- a/solution.py
+++ b/solution.py
@@ -78,6 +78,23 @@
             block = tbuf[q, g * SUB:(g + 1) * SUB, c:c + 128]
             tbuf[q, g * SUB:(g + 1) * SUB, c:c + 128] = jnp.where(label == cd_ref[:, c:c + 128], block, 0.0)
 
+    small[2].wait()
+
+    def split(c):
+        v_in[c].wait()
+
+        @pl.loop(0, chunk // 128)
+        def _(b):
+            start = pl.multiple_of(c * chunk + b * 128, 128)
+            label = jnp.broadcast_to(cd_ref[:, pl.ds(start, 128)], (128, 128)).T
+            for l in range(0, cols, 128):
+                v = jnp.where(label == ab_ref[:, l:l + 128], vraw[pl.ds(start, 128), l:l + 128], 0.0)
+                hi = v.astype(jnp.bfloat16)
+                vhi[pl.ds(start, 128), l:l + 128] = hi
+                vlo[pl.ds(start, 128), l:l + 128] = (v - hi.astype(jnp.float32)).astype(jnp.bfloat16)
+
+    split(0)
+
     others = 1 + (NX - 1) + (ny - 1) + (jnp.where(h > 0, 1, 0) if nz > 1 else 0)
     ends = jnp.where(i > 0, 1, 0) + jnp.where(i < line - 1, 1, 0)
     pl.semaphore_wait(barrier, others + ends)
@@ -164,19 +181,8 @@
         def _():
             pl.semaphore_signal(z_here, inc=1, device_id=partner, device_id_type=MESH)
 
-    small[2].wait()
-    for c in range(chunks):
-        v_in[c].wait()
-
-        @pl.loop(0, chunk // 128)
-        def _(b):
-            start = pl.multiple_of(c * chunk + b * 128, 128)
-            label = jnp.broadcast_to(cd_ref[:, pl.ds(start, 128)], (128, 128)).T
-            for l in range(0, cols, 128):
-                v = jnp.where(label == ab_ref[:, l:l + 128], vraw[pl.ds(start, 128), l:l + 128], 0.0)
-                hi = v.astype(jnp.bfloat16)
-                vhi[pl.ds(start, 128), l:l + 128] = hi
-                vlo[pl.ds(start, 128), l:l + 128] = (v - hi.astype(jnp.float32)).astype(jnp.bfloat16)
+    for c in range(1, chunks):
+        split(c)
 
     def x_copy(j, d):
         k = (x + d) % NX

time: 55.3 us -> 55.8 us (level)
  no operation moved by 1% of the time
where the time goes in v6:
time: 55.8 us; the launch traced here: 55.7 us
  Pallas kernels  54.3 us (97%)
  local copies, waits for them, and re-layouts  1.38 us (2%)
    pallas_call x1, Pallas kernels, ladder(): pl.pallas_call(functools.partial(kernel, line, ny, nz), out_shape=jax.Sha...  54.3 us
    unnamed x1, local copies, waits for them, and re-layouts  1.38 us

profile of v6, /device:TPU:224, one launch (start us, length us, event | category | flops | bytes accessed | tf_op | source)
XLA Modules:
  0.0 55.7 jit_solution(3705053456771744270)
XLA Ops:
  0.0 54.3 %shard_map.64 = f32[12,512]{1,0:T(8,128)} custom-call(f32[24,2048]{1,0:T(8,128)} %t_hbm.1, f32[2048,512]{1,0:T(8,128)} %v_hbm.1, f32[12,512]{1,0:T(8,128)} %res_hbm.1, s32[24]{0:T(128)} %ij_hbm.1, s32[1,2048]{1,0:T(1,128)} %bitcast.2, s32[1,512]{1,0:T(1,128)} %bitcast.3), custom_call_target="tpu_custom_call" | custom-call | tf_op jit(solution)/shard_map/pallas_call | solution.py:410
  54.3 1.4 %copy.8 = f32[12,512]{1,0:T(8,128)} copy(f32[12,512]{1,0:T(8,128)} %shard_map.64) | data formatting | bytes 49152
